TPU v7x, 256 devices: a whole 4x4x8 slice. The times are simulated.
256 devices in a mesh: rows: 16 (over x, y), cols: 16 (over z, core).
Axes of the slice: x: 4, y: 4, z: 8, core: 2. Of those that a mesh axis runs over, the one named last changes fastest.
Arguments:
- jacobian: float32 [32768, 192], P('rows'), may hold values from -6 to 6
- factor_cols: float32 [5, 1024, 32768], P(None, 'cols', 'rows'), may hold values from -0.13125 to 0.13125
- diag_inverse: float32 [5, 1024, 1024], P(None, 'cols'), as said below
Outputs:
- whitened: float32 [32768, 192], P('rows')
Inputs may be any that keep to these rules, and one draw needn't show every extreme that they name: Each diag_inverse[j] is lower triangular with a positive diagonal.
All inputs are finite; a program needn't handle non-finite values.
Results may differ from a plain program's by a relative error of at most 0.00011.
Values sent between devices are 32-bit elements; how exact they have to be, the bound alone decides.
A program may use at most 64 MiB of HBM per device.

v0:
```python
import jax
import jax.numpy as jnp
from jax import lax
from jax.sharding import PartitionSpec as P


def broadcast(value, axis, source):
    kept = jnp.where(lax.axis_index(axis) == source, value, 0).astype(value.dtype)
    return lax.psum(kept, axis)


def per_device(jacobian, factor_cols, diag_inverse):
    windows = diag_inverse.shape[0]
    block = diag_inverse.shape[2]
    params = jacobian.shape[1]
    owned = jacobian.shape[0] // block
    row_index = lax.axis_index("rows")
    start_blocks = jnp.asarray(jnp.arange(owned), jnp.int32)
    block_ids = row_index * owned + start_blocks
    initial = jacobian.reshape(owned, block, params)
    resid = initial
    solved = jnp.zeros((owned, block, params), jnp.float32)
    for j in range(windows):
        local = jnp.clip(j - row_index * owned, 0, owned - 1)
        current = lax.dynamic_index_in_dim(resid, local, 0, keepdims=False)
        slice_part = jnp.dot(
            diag_inverse[j],
            current,
            precision=lax.Precision.HIGHEST,
            preferred_element_type=jnp.float32,
        )
        whole = lax.all_gather(slice_part, "cols", axis=0, tiled=True)
        solved = jnp.where((block_ids == j)[:, None, None], whole[None, :, :], solved)
        shared = broadcast(slice_part, "rows", j // owned)
        update = lax.dot_general(
            factor_cols[j],
            shared,
            (((0,), (0,)), ((), ())),
            precision=lax.Precision.HIGHEST,
            preferred_element_type=jnp.float32,
        )
        update = jnp.where(
            (block_ids > j)[:, None, None], update.reshape(owned, block, params), jnp.float32(0.0)
        )
        resid = resid - lax.psum(update, "cols")
    result = jnp.where((block_ids < windows)[:, None, None], solved, resid)
    return result.reshape(owned * block, params)


def solution(mesh):
    in_specs = (P("rows", None), P(None, "cols", "rows"), P(None, "cols", None))
    out_specs = P("rows", None)
    return jax.shard_map(
        per_device, mesh=mesh, in_specs=in_specs, out_specs=out_specs, check_vma=False
    )
```

profile of v0, /device:TPU:1, one launch (start us, length us, event | category | flops | bytes accessed | tf_op | source)
XLA Modules:
  0.0 1006.0 jit_solution(7615294586444830227)
XLA Ops:
  6.5 2.6 reshape.61
  11.7 61.3 %psum.70 = f32[64,192]{1,0:T(8,128)S(1)} all-reduce(f32[64,192]{1,0:T(8,128)S(1)} %get-tuple-element.5), channel_id=1, replica_groups=mesh['rows'=16,'cols'=16] {'rows'}, use_global_device_ids=true, to_apply=%region_0.1 | all-reduce | flops 12288 | bytes 98304 | tf_op jit(solution)/shard_map/psum | solution.py:9
  73.0 2.5 convolution_bitcast_fusion.4
  75.5 2.5 reshape.62
  78.0 3.3 broadcast_select_fusion.4
  81.4 125.4 %all-reduce.6.cloned.1.call-done = f32[2,1024,192]{1,0,2:T(2,128)} async-done(((f32[2,1024,192]{1,0,2:T(2,128)}), f32[2,1024,192]{1,0,2:T(2,128)}) %all-reduce.6.cloned.1.call-update) | async-done | bytes 1572880 | tf_op jit(solution)/shard_map/psum | solution.py:45
  211.5 60.3 %psum.72 = f32[64,192]{1,0:T(8,128)S(1)} all-reduce(f32[64,192]{1,0:T(8,128)S(1)} %get-tuple-element.7), channel_id=1, replica_groups=mesh['rows'=16,'cols'=16] {'rows'}, use_global_device_ids=true, to_apply=%region_2.3 | all-reduce | flops 12288 | bytes 98304 | tf_op jit(solution)/shard_map/psum | solution.py:9
  271.8 2.5 convolution_bitcast_fusion.3
  274.3 2.5 reshape.63
  276.7 3.3 broadcast_select_fusion.3
  280.1 122.8 %all-reduce.8.cloned.1.call-done = f32[2,1024,192]{1,0,2:T(2,128)} async-done(((f32[2,1024,192]{1,0,2:T(2,128)}), f32[2,1024,192]{1,0,2:T(2,128)}) %all-reduce.8.cloned.1.call-update) | async-done | bytes 1572880 | tf_op jit(solution)/shard_map/psum | solution.py:45
  407.6 60.3 %psum.74 = f32[64,192]{1,0:T(8,128)S(1)} all-reduce(f32[64,192]{1,0:T(8,128)S(1)} %get-tuple-element.9), channel_id=1, replica_groups=mesh['rows'=16,'cols'=16] {'rows'}, use_global_device_ids=true, to_apply=%region_4.5 | all-reduce | flops 12288 | bytes 98304 | tf_op jit(solution)/shard_map/psum | solution.py:9
  467.9 2.5 convolution_bitcast_fusion.2
  470.4 2.5 reshape.64
  472.8 3.3 broadcast_select_fusion.2
  476.2 33.8 %all_gather.19 = f32[1024,192]{1,0:T(8,128)S(1)} all-gather(f32[64,192]{1,0:T(8,128)S(1)} %get-tuple-element.6), channel_id=1, replica_groups=mesh['rows'=16,'cols'=16] {'cols'}, dimensions={0}, use_global_device_ids=true | all-gather | bytes 835584 | tf_op jit(solution)/shard_map/all_gather | solution.py:32
  511.2 87.9 %all-reduce.10.cloned.1.call-done = f32[2,1024,192]{1,0,2:T(2,128)} async-done(((f32[2,1024,192]{1,0,2:T(2,128)}), f32[2,1024,192]{1,0,2:T(2,128)}) %all-reduce.10.cloned.1.call-update) | async-done | bytes 1572880 | tf_op jit(solution)/shard_map/psum | solution.py:45
  603.9 60.5 %psum.76 = f32[64,192]{1,0:T(8,128)S(1)} all-reduce(f32[64,192]{1,0:T(8,128)S(1)} %get-tuple-element.11), channel_id=1, replica_groups=mesh['rows'=16,'cols'=16] {'rows'}, use_global_device_ids=true, to_apply=%region_6.7 | all-reduce | flops 12288 | bytes 98304 | tf_op jit(solution)/shard_map/psum | solution.py:9
  664.4 2.5 convolution_bitcast_fusion.1
  666.9 2.5 reshape.65
  669.3 3.3 broadcast_select_fusion.1
  672.8 33.6 %all_gather.18 = f32[1024,192]{1,0:T(8,128)S(1)} all-gather(f32[64,192]{1,0:T(8,128)S(1)} %get-tuple-element.8), channel_id=1, replica_groups=mesh['rows'=16,'cols'=16] {'cols'}, dimensions={0}, use_global_device_ids=true | all-gather | bytes 835584 | tf_op jit(solution)/shard_map/all_gather | solution.py:32
  707.6 88.1 %all-reduce.12.cloned.1.call-done = f32[2,1024,192]{1,0,2:T(2,128)} async-done(((f32[2,1024,192]{1,0,2:T(2,128)}), f32[2,1024,192]{1,0,2:T(2,128)}) %all-reduce.12.cloned.1.call-update) | async-done | bytes 1572880 | tf_op jit(solution)/shard_map/psum | solution.py:45
  800.4 60.3 %psum.78 = f32[64,192]{1,0:T(8,128)S(1)} all-reduce(f32[64,192]{1,0:T(8,128)S(1)} %get-tuple-element.13), channel_id=1, replica_groups=mesh['rows'=16,'cols'=16] {'rows'}, use_global_device_ids=true, to_apply=%region_8.9 | all-reduce | flops 12288 | bytes 98304 | tf_op jit(solution)/shard_map/psum | solution.py:9
  860.7 2.5 convolution_bitcast_fusion
  863.2 2.5 reshape.66
  865.6 3.3 broadcast_select_fusion
  868.9 33.4 %all_gather.17 = f32[1024,192]{1,0:T(8,128)S(1)} all-gather(f32[64,192]{1,0:T(8,128)S(1)} %get-tuple-element.10), channel_id=1, replica_groups=mesh['rows'=16,'cols'=16] {'cols'}, dimensions={0}, use_global_device_ids=true | all-gather | bytes 835584 | tf_op jit(solution)/shard_map/all_gather | solution.py:32
  903.6 21.1 %all_gather.16 = f32[1024,192]{1,0:T(8,128)S(1)} all-gather(f32[64,192]{1,0:T(8,128)S(1)} %get-tuple-element.12), channel_id=1, replica_groups=mesh['rows'=16,'cols'=16] {'cols'}, dimensions={0}, use_global_device_ids=true | all-gather | bytes 835584 | tf_op jit(solution)/shard_map/all_gather | solution.py:32
  925.9 17.9 %all_gather.15 = f32[1024,192]{1,0:T(8,128)S(1)} all-gather(f32[64,192]{1,0:T(8,128)S(1)} %get-tuple-element.14), channel_id=1, replica_groups=mesh['rows'=16,'cols'=16] {'cols'}, dimensions={0}, use_global_device_ids=true | all-gather | bytes 835584 | tf_op jit(solution)/shard_map/all_gather | solution.py:32
  945.0 48.3 %all-reduce.14.cloned.1.call-done = f32[2,1024,192]{1,0,2:T(2,128)} async-done(((f32[2,1024,192]{1,0,2:T(2,128)}), f32[2,1024,192]{1,0,2:T(2,128)}) %all-reduce.14.cloned.1.call-update) | async-done | bytes 1572880 | tf_op jit(solution)/shard_map/psum | solution.py:45
  993.3 4.4 subtract_select_fusion
  (40 shorter events, 29.6 us)
Async XLA Ops:
  6.5 200.2 %all-reduce.6.cloned.1.call-start = ((), (), s32[]{:S(2)}) async-start(), calls=%async_computation | async-start | bytes 3145728 | tf_op jit(solution)/shard_map/psum | solution.py:45
  81.3 321.6 %all-reduce.8.cloned.1.call-start = ((), (), s32[]{:S(2)}) async-start(), calls=%async_computation.1 | async-start | bytes 3145728 | tf_op jit(solution)/shard_map/psum | solution.py:45
  280.0 319.1 %all-reduce.10.cloned.1.call-start = ((), (), s32[]{:S(2)}) async-start(), calls=%async_computation.2 | async-start | bytes 3145728 | tf_op jit(solution)/shard_map/psum | solution.py:45
  476.2 319.5 %all-reduce.12.cloned.1.call-start = ((), (), s32[]{:S(2)}) async-start(), calls=%async_computation.3 | async-start | bytes 3145728 | tf_op jit(solution)/shard_map/psum | solution.py:45
  672.6 320.6 %all-reduce.14.cloned.1.call-start = ((), (), s32[]{:S(2)}) async-start(), calls=%async_computation.4 | async-start | bytes 3145728 | tf_op jit(solution)/shard_map/psum | solution.py:45
  925.9 67.4 %copy-start = (f32[1024,192]{0,1:T(8,128)S(1)}, f32[1024,192]{0,1:T(8,128)}, u32[]{:S(2)}) copy-start(f32[1024,192]{0,1:T(8,128)} %copy.8) | copy-start | bytes 2359300
Sparse Core Ops, SparseCore 0:
  81.4 125.2 all-reduce.5
  280.2 122.6 all-reduce.7
  476.3 122.8 all-reduce.9
  672.8 122.8 all-reduce.11
  869.1 124.1 all-reduce.13
where the time goes:
time: 1010 us
  waiting for transfers between devices  473 us (47%)
  blocking collectives  442 us (44%)
  other arithmetic  29.8 us (3%)
  local copies, waits for them, and re-layouts  26.2 us (3%)
  matrix products  21.6 us (2%)
  between operations  13.3 us (1%)
    psum x5, waiting for transfers between devices, per_device(): resid = resid - lax.psum(update, 'cols')  472 us
    psum x5, blocking collectives, broadcast(): return lax.psum(kept, axis)  303 us
    all_gather x5, blocking collectives, per_device(): whole = lax.all_gather(slice_part, 'cols', axis=0, tiled=True)  140 us
  transfers between devices with their start and end apart: 5, of which 5 were waited for; matrix products, arithmetic and copies ran while one was open for 1% of the time, Pallas kernels for 0%

commit v1 on v0

v1 whole, which is shorter than its diff:
```python
import jax
import jax.numpy as jnp
from jax import lax
from jax.experimental import pallas as pl
from jax.experimental.pallas import tpu as pltpu
from jax.sharding import PartitionSpec as P

MESH = pl.DeviceIdType.MESH
NT = (((1,), (1,)), ((), ()))
NN = (((1,), (0,)), ((), ()))


def halves(a):
    hi = a.astype(jnp.bfloat16)
    lo = (a - hi.astype(jnp.float32)).astype(jnp.bfloat16)
    return hi, lo


def dot3(a, b, dims):
    ah, al = halves(a)
    bh, bl = halves(b)

    def one(p, q):
        return lax.dot_general(p, q, dims, preferred_element_type=jnp.float32)

    return one(ah, bh) + (one(ah, bl) + one(al, bh))


def lanes(i, n=128):
    return pl.ds(pl.multiple_of(i * n, n), n)


def subl(i, n):
    return pl.ds(pl.multiple_of(i * n, n), n)


def kernel(
    jac, fac, dinv, out,
    dv, fv, jv, jt, jsv, js, x0, t1, ts, tp, xf, lt2, lt3, lt4, jtile,
    pa, ss, sb, u, rsend, rbuf,
    load_sem, pair_send, pair_recv, own_send, own_recv, fwd_send, fwd_recv,
    a_send, a_recv, b_send, b_recv, h_send, h_recv, r_send, r_recv, g_send, g_recv, o_send, o_recv,
):
    r = lax.axis_index("rows")
    c = lax.axis_index("cols")
    x = r // 4
    y = r % 4
    z = c // 2
    core = c % 2
    h = y // 2
    g = x * 2 + y % 2

    def zdev(d):
        return {"cols": ((z + d + 8) % 8) * 2 + core}

    def rdev(d):
        return {"rows": (r + d) % 16}

    partner = {"cols": c + 1 - 2 * core}
    hdev = {"rows": x * 4 + 3 - y}

    def remote(src, dst, ssem, rsem, dev):
        return pltpu.make_async_remote_copy(
            src_ref=src, dst_ref=dst, send_sem=ssem, recv_sem=rsem, device_id=dev, device_id_type=MESH
        )

    sent = []

    mine = subl(core, 64)
    load_d = pltpu.make_async_copy(dinv, dv.at[:, mine, :], load_sem.at[0])
    load_d.start()
    load_f = pltpu.make_async_copy(fac, fv.at[:, mine, :], load_sem.at[1])
    load_f.start()
    load_j = [
        pltpu.make_async_copy(jac.at[pl.ds(b * 1024 + pl.multiple_of(z * 128, 128), 128), :], jsv.at[b], load_sem.at[2 + b])
        for b in range(2)
    ]
    for cp in load_j:
        cp.start()

    @pl.when(r <= 2)
    def _():
        pltpu.make_async_copy(jac, jv, load_sem.at[4]).start()

    bar = pltpu.get_barrier_semaphore()
    for d in range(1, 16):
        pl.semaphore_signal(bar, inc=1, device_id=rdev(d), device_id_type=MESH)
    for d in range(1, 8):
        pl.semaphore_signal(bar, inc=1, device_id=zdev(d), device_id_type=MESH)
    pl.semaphore_signal(bar, inc=1, device_id=partner, device_id_type=MESH)
    pl.semaphore_wait(bar, 23)

    pair = []
    for i, (src, dst) in enumerate(
        (
            (dinv.at[0], dv.at[0, mine, :]),
            (fac.at[0], fv.at[0, mine, :]),
            (dinv.at[pl.ds(1, 4)], dv.at[pl.ds(1, 4), mine, :]),
            (fac.at[pl.ds(1, 4)], fv.at[pl.ds(1, 4), mine, :]),
        )
    ):
        cp = remote(src, dst, pair_send.at[i], pair_recv.at[i], partner)
        cp.start()
        pair.append(cp)
        sent.append(cp)

    lts = {2: lt2, 3: lt3, 4: lt4}

    def tile_copies(j, d):
        to = (r + d) % 16
        tx = to // 4
        ty = to % 4
        tg = tx * 2 + ty % 2
        th = ty // 2
        rows = pl.ds(pl.multiple_of((j % 2) * 1024 + tg * 128, 128), 128)
        a_src, a_dst = fac.at[pl.ds(0, j), :, rows], lts[j].at[:, mine, :]
        j_src = jt.at[j % 2, pl.ds(pl.multiple_of(core * 96 + th * 48, 48), 48), lanes(tg)]
        j_dst = jtile.at[j]
        return (a_src, a_dst), (j_src, j_dst)

    def send_fac(j):
        for d in range(1, 16):
            (s, t), _ = tile_copies(j, d)
            remote(s, t, own_send.at[j, 0, d], own_recv.at[j, 0], rdev(d)).start()
        (s, t), _ = tile_copies(j, 0)
        pltpu.make_async_copy(s, t, own_recv.at[j, 0]).start()

    def send_jac(j):
        for d in range(1, 16):
            _, (s, t) = tile_copies(j, d)
            remote(s, t, own_send.at[j, 1, d], own_recv.at[j, 1], rdev(d)).start()
        _, (s, t) = tile_copies(j, 0)
        pltpu.make_async_copy(s, t, own_recv.at[j, 1]).start()

    def wait_fac(j):
        pltpu.make_async_copy(lts[j].at[:, mine, :], lts[j].at[:, mine, :], own_recv.at[j, 0]).wait()

    def wait_jac(j):
        pltpu.make_async_copy(jtile.at[j], jtile.at[j], own_recv.at[j, 1]).wait()

    def wait_owner_sends(j):
        for d in range(1, 16):
            (s, t), (s2, t2) = tile_copies(j, d)
            remote(s, t, own_send.at[j, 0, d], own_recv.at[j, 0], rdev(d)).wait_send()
            remote(s2, t2, own_send.at[j, 1, d], own_recv.at[j, 1], rdev(d)).wait_send()

    @pl.when(r == 1)
    def _():
        send_fac(2)
        send_fac(3)

    @pl.when(r == 2)
    def _():
        send_fac(4)

    @pl.when(r <= 2)
    def _():
        pltpu.make_async_copy(jac, jv, load_sem.at[4]).wait()
        jt[0] = jv[0:1024, :].T

    @pl.when(r == 2)
    def _():
        send_jac(4)

    load_d.wait()
    load_f.wait()
    pair[0].wait_recv()
    pair[1].wait_recv()

    half = subl(core, 96)
    quarter = subl(h, 48)

    def t1_copy(d):
        to = (r + d) % 16
        tx = to // 4
        ty = to % 4
        tg = tx * 2 + ty % 2
        th = ty // 2
        return remote(
            t1.at[pl.ds(pl.multiple_of(th * 48, 48), 48), lanes(tg)], ts.at[1], own_send.at[0, 0, d], own_recv.at[0, 0], rdev(d)
        )

    def x0_copy(d):
        return remote(x0, xf.at[0], own_send.at[0, 1, d], own_recv.at[0, 1], rdev(d))

    @pl.when(r == 0)
    def _():
        first = dot3(jt[0, half, :], dv[0], NT)
        x0[...] = first
        t1[...] = dot3(first, fv[0, :, 1024:2048], NN)
        jt[1] = jv[1024:2048, :].T

        @pl.when(z == 0)
        def _():
            t1[...] = t1[...] - jt[1, half, :]

        for d in range(1, 16):
            t1_copy(d).start()
        for d in range(1, 16):
            x0_copy(d).start()
        ts[1] = t1[0:48, 0:128]
        xf[0] = x0[...]

    @pl.when(r == 1)
    def _():
        send_jac(2)
        jt[1] = jv[1024:2048, :].T
        send_jac(3)

    for b in range(2):
        load_j[b].wait()
        js[b] = jsv[b].T

    @pl.when(r != 0)
    def _():
        pltpu.make_async_copy(ts.at[1], ts.at[1], own_recv.at[0, 0]).wait()

    def forward(j):
        wait_fac(j)
        cp = remote(lts[j].at[:, mine, :], lts[j].at[:, mine, :], fwd_send.at[j], fwd_recv.at[j], partner)
        cp.start()
        sent.append(cp)
        return cp

    fwd = {}
    swap = {}

    def update(j):
        if j == 0:
            @pl.when(r != 0)
            def _():
                pltpu.make_async_copy(xf.at[0], xf.at[0], own_recv.at[0, 1]).wait()
        else:
            swap[j].wait_recv()
        if j == 1:
            pair[3].wait_recv()
        for b in range(2):
            part = dot3(xf[j], fv[j, :, b * 1024:(b + 1) * 1024], NN)
            if j == 0:
                u[b] = part
            else:
                u[b] = u[b] + part

    for j in range(1, 5):
        stage = []
        for d in (4, 3, 5, 2, 6, 1, 7):
            cp = remote(ts.at[j], pa.at[j - 1, d - 1], a_send.at[j - 1, d], a_recv.at[j - 1, d], zdev(d))
            cp.start()
            stage.append(cp)
        sent.extend(stage)
        if j == 1:
            fwd[2] = forward(2)
        if j == 2:
            fwd[4] = forward(4)
        update(j - 1)
        for cp in stage:
            cp.wait_recv()
        total = ts[j]
        for d in range(7):
            total = total + pa[j - 1, d]
        if j == 1:
            rest = -total
        else:
            wait_jac(j)
            rest = jtile[j] - total
        ss[j - 1] = rest
        sb[j - 1, :, lanes(g)] = rest
        stage = []
        for dx in (2, 1, 3, 0):
            for dy in (1, 0):
                if dx == 0 and dy == 0:
                    continue
                ny = h * 2 + (y % 2 + dy) % 2
                to = {"rows": ((x + dx) % 4) * 4 + ny}
                k = dx * 2 + dy
                cp = remote(ss.at[j - 1], sb.at[j - 1, :, lanes(g)], b_send.at[j - 1, k], b_recv.at[j - 1, k], to)
                cp.start()
                stage.append(cp)
        sent.extend(stage)
        if j == 1:
            fwd[3] = forward(3)
        if j < 4:
            fwd[j + 1].wait_recv()
            part = dot3(xf[0, quarter, :], lts[j + 1][0], NN)
            for m in range(1, j):
                part = part + dot3(xf[m, quarter, :], lts[j + 1][m], NN)
            tp[...] = part
        if j == 1:
            pair[2].wait_recv()
        for cp in stage:
            cp.wait_recv()
        new = dot3(sb[j - 1], dv[j], NT)
        xf[j, quarter, :] = new
        if j < 4:
            ts[j + 1] = tp[...] + dot3(new, lts[j + 1][j], NN)
        cp = remote(xf.at[j, quarter, :], xf.at[j, quarter, :], h_send.at[j], h_recv.at[j], hdev)
        cp.start()
        sent.append(cp)
        swap[j] = cp

    update(4)

    paths = ((0, -1, 4), (1, 1, 4), (0, 1, 3), (1, -1, 3))
    got = [None] * 4
    for s in range(4):
        for i, (b, way, hops) in enumerate(paths):
            if s >= hops:
                continue
            target = (z + way * (hops - s) + 8) % 8
            value = u[b, :, lanes(target)]
            if s > 0:
                got[i].wait_recv()
                value = value + rbuf[i, s - 1]
            rsend[i, s] = value
            cp = remote(rsend.at[i, s], rbuf.at[i, s], r_send.at[i, s], r_recv.at[i, s], zdev(way))
            cp.start()
            sent.append(cp)
            got[i] = cp

    def piece(b, origin):
        return out.at[b, half, lanes(origin)]

    gather = {}
    last = []

    def share(b, origin, k):
        cp = remote(piece(b, origin), piece(b, origin), o_send.at[k], o_recv.at[k], partner)
        cp.start()
        sent.append(cp)
        last.append(cp)

    def hop(i, s):
        b, way, hops = gpaths[i]
        origin = (z - way * s + 8) % 8
        cp = remote(piece(b, origin), piece(b, origin), g_send.at[i, s], g_recv.at[i, s], zdev(way))
        cp.start()
        sent.append(cp)
        gather[i] = cp

    gpaths = ((0, 1, 4), (1, -1, 4), (0, -1, 3), (1, 1, 3))
    for b in range(2):
        for i, (pb, way, hops) in enumerate(paths):
            if pb == b:
                got[i].wait_recv()
        first, second = [i for i in range(4) if paths[i][0] == b]
        total = u[b, :, lanes(z)] + rbuf[first, paths[first][2] - 1] + rbuf[second, paths[second][2] - 1]
        block = r * 2 + b
        solved = xf[jnp.minimum(block, 4)]
        updated = js[b, half, :] - total
        out[b, half, lanes(z)] = jnp.where(block < 5, solved, updated)
        for i in range(4):
            if gpaths[i][0] == b:
                hop(i, 0)
        share(b, z, b)
    k = 2
    for s in range(1, 5):
        for i in range(4):
            b, way, hops = gpaths[i]
            if s > hops:
                continue
            gather[i].wait_recv()
            if s < hops:
                hop(i, s)
            share(b, (z - way * s + 8) % 8, k)
            k += 1
    for cp in last:
        cp.wait_recv()
    for cp in sent:
        cp.wait_send()

    @pl.when(r == 0)
    def _():
        for d in range(1, 16):
            t1_copy(d).wait_send()
            x0_copy(d).wait_send()

    @pl.when(r == 1)
    def _():
        wait_owner_sends(2)
        wait_owner_sends(3)

    @pl.when(r == 2)
    def _():
        wait_owner_sends(4)


def per_device(jacobian, factor_cols, diag_inverse):
    f32 = jnp.float32
    dma = pltpu.SemaphoreType.DMA
    out = pl.pallas_call(
        kernel,
        out_shape=jax.ShapeDtypeStruct((2, 192, 1024), f32),
        in_specs=[pl.BlockSpec(memory_space=pl.ANY)] * 3,
        out_specs=pl.BlockSpec(memory_space=pltpu.VMEM),
        scratch_shapes=[
            pltpu.VMEM((5, 128, 1024), f32),
            pltpu.VMEM((5, 128, 2048), f32),
            pltpu.VMEM((2048, 192), f32),
            pltpu.VMEM((2, 192, 1024), f32),
            pltpu.VMEM((2, 128, 192), f32),
            pltpu.VMEM((2, 192, 128), f32),
            pltpu.VMEM((96, 128), f32),
            pltpu.VMEM((96, 1024), f32),
            pltpu.VMEM((5, 48, 128), f32),
            pltpu.VMEM((48, 128), f32),
            pltpu.VMEM((5, 96, 128), f32),
            pltpu.VMEM((2, 128, 128), f32),
            pltpu.VMEM((3, 128, 128), f32),
            pltpu.VMEM((4, 128, 128), f32),
            pltpu.VMEM((5, 48, 128), f32),
            pltpu.VMEM((4, 7, 48, 128), f32),
            pltpu.VMEM((4, 48, 128), f32),
            pltpu.VMEM((4, 48, 1024), f32),
            pltpu.VMEM((2, 96, 1024), f32),
            pltpu.VMEM((4, 4, 96, 128), f32),
            pltpu.VMEM((4, 4, 96, 128), f32),
            dma((5,)),
            dma((4,)), dma((4,)),
            dma((5, 2, 16)), dma((5, 2)),
            dma((5,)), dma((5,)),
            dma((4, 8)), dma((4, 8)),
            dma((4, 8)), dma((4, 8)),
            dma((5,)), dma((5,)),
            dma((4, 4)), dma((4, 4)),
            dma((4, 4)), dma((4, 4)),
            dma((16,)), dma((16,)),
        ],
        compiler_params=pltpu.CompilerParams(
            collective_id=0, has_side_effects=True, vmem_limit_bytes=48 * 1024 * 1024
        ),
        name="whiten",
    )(jacobian, factor_cols, diag_inverse)
    return jnp.transpose(out, (0, 2, 1)).reshape(2048, 192)


def solution(mesh):
    in_specs = (P("rows", None), P(None, "cols", "rows"), P(None, "cols", None))
    return jax.shard_map(
        per_device, mesh=mesh, in_specs=in_specs, out_specs=P("rows", None), check_vma=False
    )
```

time: 1010 us -> 121 us (0.12)
  waiting for transfers between devices: 473 us -> 0 us
  blocking collectives: 442 us -> 0 us
  Pallas kernels: 0 us -> 118 us
  other arithmetic: 29.8 us -> 0 us
  local copies, waits for them, and re-layouts: 26.2 us -> 3.26 us
  matrix products: 21.6 us -> 0 us
  between operations: 13.3 us -> 0.03 us
    psum x5 -> x0, waiting for transfers between devices: 472 us -> none  [per_device(): resid = resid - lax.psum(update, 'cols')]
    psum x5 -> x0, blocking collectives: 303 us -> none  [broadcast(): return lax.psum(kept, axis)]
    all_gather x5 -> x0, blocking collectives: 140 us -> none  [per_device(): whole = lax.all_gather(slice_part, 'cols', axis=0, tiled=True)]
    pallas_call x0 -> x1, Pallas kernels: none -> 118 us  [per_device(): pl.pallas_call(kernel, out_shape=jax.ShapeDtypeStruct((2, 192, 1024), f32...]
    dot_general x10 -> x0, matrix products: 21.6 us -> none  [the longest x5 12.3 us: per_device(): lax.dot_general(factor_cols[j], shared, (((0,), (0,)), ((), ())), precisi...]
    select_n x6 -> x0, other arithmetic: 20.9 us -> none  [the longest x5 16.4 us: per_device(): jnp.where((block_ids > j)[:, None, None], update.reshape(owned, block, pa...]
    reshape x6 -> x1, local copies, waits for them, and re-layouts: 15 us -> 1.32 us  [per_device(): return jnp.transpose(out, (0, 2, 1)).reshape(2048, 192)]
  transfers between devices with their start and end apart: 5 -> 0, of which waited for: 5 -> 0; matrix products, arithmetic and copies ran while one was open for 1% -> 0% of each run, Pallas kernels for 0% -> 0%
where the time goes in v1:
time: 121 us
  Pallas kernels  118 us (98%)
  local copies, waits for them, and re-layouts  3.26 us (3%)
    pallas_call x1, Pallas kernels, per_device(): pl.pallas_call(kernel, out_shape=jax.ShapeDtypeStruct((2, 192, 1024), f32...  118 us

profile of v1, /device:TPU:1, one launch (start us, length us, event | category | flops | bytes accessed | tf_op | source)
XLA Modules:
  0.0 121.3 jit_solution(9499683652931012090)
XLA Ops:
  0.0 0.0 copy-start
  0.0 1.9 %copy.5.jac = f32[2048,192]{1,0:T(8,128)S(1)} copy(f32[2048,192]{0,1:T(8,128)} %param.3) | data formatting | bytes 3145728 | tf_op args[0]
  1.9 0.0 copy-done
  2.0 118.0 %whiten.1 = f32[2,192,1024]{2,1,0:T(8,128)S(1)} custom-call(f32[2048,192]{1,0:T(8,128)S(1)} %copy.5.jac, f32[5,64,2048]{2,1,0:T(8,128)} %fac.1, f32[5,64,1024]{2,1,0:T(8,128)S(1)} %copy-done), custom_call_target="tpu_custom_call" | custom-call | tf_op jit(solution)/shard_map/whiten/pallas_call | solution.py:390
  120.0 1.3 %copy.7 = f32[2,24,8,1024]{3,2,0,1:T(8,128)} copy(f32[2,24,8,1024]{3,2,1,0:T(8,128)S(1)} %bitcast.3) | data formatting | bytes 3145728 | tf_op jit(solution)/shard_map/reshape | solution.py:433
Async XLA Ops:
  0.0 1.9 %copy-start = (f32[5,64,1024]{2,1,0:T(8,128)S(1)}, f32[5,64,1024]{2,1,0:T(8,128)}, u32[]{:S(2)}) copy-start(f32[5,64,1024]{2,1,0:T(8,128)} %dinv.1) | copy-start | bytes 3932164

commit v2 on v1

v2 whole, which is shorter than its diff:
```python
import jax
import jax.numpy as jnp
from jax import lax
from jax.experimental import pallas as pl
from jax.experimental.pallas import tpu as pltpu
from jax.sharding import PartitionSpec as P

MESH = pl.DeviceIdType.MESH
FAR = (10, 8, 9, 11, 6, 5, 7, 4, 14, 13, 15, 12, 2, 1, 3)
NT = (((1,), (1,)), ((), ()))
NN = (((1,), (0,)), ((), ()))


def halves(a):
    hi = a.astype(jnp.bfloat16)
    lo = (a - hi.astype(jnp.float32)).astype(jnp.bfloat16)
    return hi, lo


def dot3(a, b, dims):
    ah, al = halves(a)
    bh, bl = halves(b)

    def one(p, q):
        return lax.dot_general(p, q, dims, preferred_element_type=jnp.float32)

    return one(ah, bh) + (one(ah, bl) + one(al, bh))


def lanes(i, n=128):
    return pl.ds(pl.multiple_of(i * n, n), n)


def subl(i, n):
    return pl.ds(pl.multiple_of(i * n, n), n)


def kernel(
    jac, fac, dinv, out,
    dv, fv, jt, js, x0, t1, ts, tp, xf, lt2, lt3, lt4, jtile,
    pa, ss, sb, u, rsend, rbuf,
    load_sem, pair_send, pair_recv, own_send, own_recv, fwd_send, fwd_recv, pass_send, pass_recv,
    a_send, a_recv, b_send, b_recv, h_send, h_recv, r_send, r_recv, g_send, g_recv, o_send, o_recv,
):
    r = lax.axis_index("rows")
    c = lax.axis_index("cols")
    x = r // 4
    y = r % 4
    z = c // 2
    core = c % 2
    h = y // 2
    g = x * 2 + (y + h) % 2

    def zdev(d):
        return {"cols": ((z + d + 8) % 8) * 2 + core}

    def rdev(d):
        return {"rows": (r + d) % 16}

    partner = {"cols": c + 1 - 2 * core}
    hdev = {"rows": x * 4 + 3 - y}

    def remote(src, dst, ssem, rsem, dev):
        return pltpu.make_async_remote_copy(
            src_ref=src, dst_ref=dst, send_sem=ssem, recv_sem=rsem, device_id=dev, device_id_type=MESH
        )

    sent = []

    mine = subl(core, 64)
    first_rows = pl.ds(1024, 1024)
    load_0 = [
        pltpu.make_async_copy(dinv.at[0], dv.at[0, mine, :], load_sem.at[0]),
        pltpu.make_async_copy(fac.at[0, :, first_rows], fv.at[0, mine, first_rows], load_sem.at[1]),
    ]
    load_d = pltpu.make_async_copy(dinv.at[pl.ds(1, 4)], dv.at[pl.ds(1, 4), mine, :], load_sem.at[5])
    load_f = pltpu.make_async_copy(fac.at[pl.ds(1, 4)], fv.at[pl.ds(1, 4), mine, :], load_sem.at[6])
    load_g = pltpu.make_async_copy(fac.at[0, :, pl.ds(0, 1024)], fv.at[0, mine, pl.ds(0, 1024)], load_sem.at[7])
    for cp in load_0:
        cp.start()
    load_j = [
        pltpu.make_async_copy(
            jac.at[subl(core, 96), pl.ds(pl.multiple_of(b * 1024 + z * 128, 128), 128)], js.at[b], load_sem.at[2 + b]
        )
        for b in range(2)
    ]
    for cp in load_j:
        cp.start()

    load_jt = pltpu.make_async_copy(jac.at[subl(core, 96), :], jt, load_sem.at[4])

    @pl.when(r == 0)
    def _():
        load_jt.start()

    bar = pltpu.get_barrier_semaphore()
    for d in range(1, 16):
        pl.semaphore_signal(bar, inc=1, device_id=rdev(d), device_id_type=MESH)
    for d in range(1, 8):
        pl.semaphore_signal(bar, inc=1, device_id=zdev(d), device_id_type=MESH)
    pl.semaphore_signal(bar, inc=1, device_id=partner, device_id_type=MESH)
    pl.semaphore_wait(bar, 23)

    pair = [
        remote(src, dst, pair_send.at[i], pair_recv.at[i], partner)
        for i, (src, dst) in enumerate(
            (
                (dinv.at[0], dv.at[0, mine, :]),
                (fac.at[0, :, first_rows], fv.at[0, mine, first_rows]),
                (dinv.at[pl.ds(1, 4)], dv.at[pl.ds(1, 4), mine, :]),
                (fac.at[pl.ds(1, 4)], fv.at[pl.ds(1, 4), mine, :]),
                (fac.at[0, :, pl.ds(0, 1024)], fv.at[0, mine, pl.ds(0, 1024)]),
            )
        )
    ]
    for cp in pair[:2]:
        cp.start()
        sent.append(cp)

    lts = {2: lt2, 3: lt3, 4: lt4}
    owner_h = {2: 0, 3: 0, 4: 1}

    def fac_copy(j, k):
        tx = (x + k // 2) % 4
        ty = h * 2 + (y % 2 + k % 2) % 2
        tg = tx * 2 + (ty + h) % 2
        rows = pl.ds(pl.multiple_of((j % 2) * 1024 + tg * 128, 128), 128)
        src, dst = fac.at[pl.ds(0, j), :, rows], lts[j].at[:, mine, :]
        if k == 0:
            return pltpu.make_async_copy(src, dst, own_recv.at[j, 0])
        return remote(src, dst, own_send.at[j, 0, k], own_recv.at[j, 0], {"rows": tx * 4 + ty})

    def jac_copy(j, d):
        to = (r + d) % 16
        tx = to // 4
        ty = to % 4
        th = ty // 2
        tg = tx * 2 + (ty + th) % 2
        rows = pl.ds(pl.multiple_of((j % 2) * 1024 + tg * 128, 128), 128)
        src = jac.at[pl.ds(pl.multiple_of(core * 96 + th * 48 + z * 8, 8), 8), rows]
        if d == 0:
            return pltpu.make_async_copy(src, jtile.at[j], own_recv.at[j, 1])
        return remote(src, jtile.at[j], own_send.at[j, 1, d], own_recv.at[j, 1], rdev(d))

    def send_fac(j):
        for k in (4, 5, 2, 3, 6, 7, 1, 0):
            fac_copy(j, k).start()

    def send_jac(j):
        @pl.when(z < 6)
        def _():
            for d in range(16):
                jac_copy(j, d).start()

    def wait_fac(j):
        @pl.when(h == owner_h[j])
        def _():
            pltpu.make_async_copy(lts[j].at[:, mine, :], lts[j].at[:, mine, :], own_recv.at[j, 0]).wait()
            fac_pass(j).start()

        @pl.when(h != owner_h[j])
        def _():
            fac_pass(j).wait_recv()

    def fac_pass(j):
        return remote(lts[j].at[:, mine, :], lts[j].at[:, mine, :], pass_send.at[j], pass_recv.at[j], hdev)

    def wait_jac(j):
        @pl.when(z < 6)
        def _():
            pltpu.make_async_copy(jtile.at[j], jtile.at[j], own_recv.at[j, 1]).wait()

    def wait_owner_sends(j):
        for k in range(1, 8):
            fac_copy(j, k).wait_send()

        @pl.when(z < 6)
        def _():
            for d in range(1, 16):
                jac_copy(j, d).wait_send()

    @pl.when(r == 1)
    def _():
        send_fac(2)
        send_jac(2)
        send_fac(3)
        send_jac(3)

    @pl.when(r == 2)
    def _():
        send_fac(4)
        send_jac(4)

    for cp in load_0:
        cp.wait()
    for cp in pair[:2]:
        cp.wait_recv()

    half = subl(core, 96)
    quarter = subl(h, 48)

    def first_copy(d):
        to = (r + d) % 16
        tx = to // 4
        ty = to % 4
        th = ty // 2
        tg = tx * 2 + (ty + th) % 2
        rows = pl.ds(pl.multiple_of(th * 48, 48), 48)
        t1_cp = remote(t1.at[tg, rows], ts.at[1], own_send.at[0, 0, d], own_recv.at[0, 0], rdev(d))
        x0_cp = remote(x0.at[rows], xf.at[0, rows], own_send.at[0, 1, d], own_recv.at[0, 1], rdev(d))
        return t1_cp, x0_cp

    @pl.when(r == 0)
    def _():
        load_jt.wait()
        first = dot3(jt[:, 0:1024], dv[0], NT)
        x0[...] = first
        whole = dot3(first, fv[0, :, 1024:2048], NN)
        for i in range(8):
            t1[i] = whole[:, i * 128:(i + 1) * 128]

        @pl.when(z == 0)
        def _():
            for i in range(8):
                t1[i] = t1[i] - jt[:, 1024 + i * 128:1024 + (i + 1) * 128]

        for d in FAR:
            first_copy(d)[0].start()
        for d in FAR:
            first_copy(d)[1].start()
        ts[1] = t1[0, 0:48]
        xf[0, 0:48] = x0[0:48]

    for cp in pair[2:]:
        cp.start()
        sent.append(cp)
    for cp in (load_d, load_f, load_g):
        cp.start()
    for cp in load_j:
        cp.wait()

    @pl.when(r != 0)
    def _():
        pltpu.make_async_copy(ts.at[1], ts.at[1], own_recv.at[0, 0]).wait()

    def forward(j):
        wait_fac(j)
        cp = remote(lts[j].at[:, mine, :], lts[j].at[:, mine, :], fwd_send.at[j], fwd_recv.at[j], partner)
        cp.start()
        sent.append(cp)
        return cp

    fwd = {}
    swap = {}

    def exchange(j):
        cp = remote(xf.at[j, quarter, :], xf.at[j, quarter, :], h_send.at[j], h_recv.at[j], hdev)
        cp.start()
        sent.append(cp)
        swap[j] = cp

    def update(j):
        swap[j].wait_recv()
        if j == 0:
            for cp in (load_f, load_g):
                cp.wait()
            for cp in pair[3:]:
                cp.wait_recv()
        for b in range(2):
            part = dot3(xf[j], fv[j, :, b * 1024:(b + 1) * 1024], NN)
            for i in range(8):
                piece = part[:, i * 128:(i + 1) * 128]
                u[b, i] = piece if j == 0 else u[b, i] + piece

    for j in range(1, 5):
        stage = []
        for d in (4, 3, 5, 2, 6, 1, 7):
            cp = remote(ts.at[j], pa.at[j - 1, d - 1], a_send.at[j - 1, d], a_recv.at[j - 1, d], zdev(d))
            cp.start()
            stage.append(cp)
        sent.extend(stage)
        if j == 1:
            fwd[2] = forward(2)

            @pl.when(r != 0)
            def _():
                pltpu.make_async_copy(xf.at[0, quarter], xf.at[0, quarter], own_recv.at[0, 1]).wait()

            exchange(0)
        if j == 2:
            fwd[4] = forward(4)
            update(0)
        if j > 1:
            update(j - 1)
        for cp in stage:
            cp.wait_recv()
        total = ts[j]
        for d in range(7):
            total = total + pa[j - 1, d]
        rest = -total
        ss[j - 1] = rest
        sb[j - 1, g] = rest
        stage = []
        for dx in (2, 1, 3, 0):
            for dy in (1, 0):
                if dx == 0 and dy == 0:
                    continue
                ny = h * 2 + (y + dy) % 2
                to = {"rows": ((x + dx) % 4) * 4 + ny}
                k = dx * 2 + dy
                cp = remote(ss.at[j - 1], sb.at[j - 1, g], b_send.at[j - 1, k], b_recv.at[j - 1, k], to)
                cp.start()
                stage.append(cp)
        sent.extend(stage)
        if j == 1:
            fwd[3] = forward(3)
        if j < 4:
            fwd[j + 1].wait_recv()
            part = dot3(xf[0, quarter, :], lts[j + 1][0], NN)
            for m in range(1, j):
                part = part + dot3(xf[m, quarter, :], lts[j + 1][m], NN)
            tp[...] = part
        if j == 1:
            load_d.wait()
            pair[2].wait_recv()
        for cp in stage:
            cp.wait_recv()
        new = dot3(jnp.concatenate([sb[j - 1, i] for i in range(8)], axis=1), dv[j], NT)
        xf[j, quarter, :] = new
        if j < 4:
            ts[j + 1] = tp[...] + dot3(new, lts[j + 1][j], NN)
            wait_jac(j + 1)

            @pl.when(z < 6)
            def _():
                ts[j + 1, subl(z, 8)] = ts[j + 1, subl(z, 8)] - jtile[j + 1]
        exchange(j)

    update(4)

    paths = ((0, -1, 4), (1, 1, 4), (0, 1, 3), (1, -1, 3))
    got = [None] * 4
    for s in range(4):
        for i, (b, way, hops) in enumerate(paths):
            if s >= hops:
                continue
            target = (z + way * (hops - s) + 8) % 8
            value = u[b, target]
            if s > 0:
                got[i].wait_recv()
                value = value + rbuf[i, s - 1]
            rsend[i, s] = value
            cp = remote(rsend.at[i, s], rbuf.at[i, s], r_send.at[i, s], r_recv.at[i, s], zdev(way))
            cp.start()
            sent.append(cp)
            got[i] = cp

    def piece(b, origin):
        return out.at[b * 8 + origin, half]

    gather = {}
    last = []

    def share(b, origin, k):
        cp = remote(piece(b, origin), piece(b, origin), o_send.at[k], o_recv.at[k], partner)
        cp.start()
        sent.append(cp)
        last.append(cp)

    def hop(i, s):
        b, way, hops = gpaths[i]
        origin = (z - way * s + 8) % 8
        cp = remote(piece(b, origin), piece(b, origin), g_send.at[i, s], g_recv.at[i, s], zdev(way))
        cp.start()
        sent.append(cp)
        gather[i] = cp

    gpaths = ((0, 1, 4), (1, -1, 4), (0, -1, 3), (1, 1, 3))
    for b in range(2):
        for i, (pb, way, hops) in enumerate(paths):
            if pb == b:
                got[i].wait_recv()
        first, second = [i for i in range(4) if paths[i][0] == b]
        total = u[b, z] + rbuf[first, paths[first][2] - 1] + rbuf[second, paths[second][2] - 1]
        block = r * 2 + b
        solved = xf[jnp.minimum(block, 4)]
        updated = js[b] - total
        out[b * 8 + z, half] = jnp.where(block < 5, solved, updated)
        for i in range(4):
            if gpaths[i][0] == b:
                hop(i, 0)
        share(b, z, b)
    k = 2
    for s in range(1, 5):
        for i in range(4):
            b, way, hops = gpaths[i]
            if s > hops:
                continue
            gather[i].wait_recv()
            if s < hops:
                hop(i, s)
            share(b, (z - way * s + 8) % 8, k)
            k += 1
    for cp in last:
        cp.wait_recv()
    for cp in sent:
        cp.wait_send()

    @pl.when(r == 0)
    def _():
        for d in range(1, 16):
            for cp in first_copy(d):
                cp.wait_send()

    @pl.when(r == 1)
    def _():
        wait_owner_sends(2)
        wait_owner_sends(3)

    @pl.when(r == 2)
    def _():
        wait_owner_sends(4)

    for j in (2, 3, 4):
        @pl.when(h == owner_h[j])
        def _():
            fac_pass(j).wait_send()


def per_device(jacobian, factor_cols, diag_inverse):
    f32 = jnp.float32
    dma = pltpu.SemaphoreType.DMA
    out = pl.pallas_call(
        kernel,
        out_shape=jax.ShapeDtypeStruct((16, 192, 128), f32),
        in_specs=[pl.BlockSpec(memory_space=pl.ANY)] * 3,
        out_specs=pl.BlockSpec(memory_space=pltpu.VMEM),
        scratch_shapes=[
            pltpu.VMEM((5, 128, 1024), f32),
            pltpu.VMEM((5, 128, 2048), f32),
            pltpu.VMEM((96, 2048), f32),
            pltpu.VMEM((2, 96, 128), f32),
            pltpu.VMEM((96, 128), f32),
            pltpu.VMEM((8, 96, 128), f32),
            pltpu.VMEM((5, 48, 128), f32),
            pltpu.VMEM((48, 128), f32),
            pltpu.VMEM((5, 96, 128), f32),
            pltpu.VMEM((2, 128, 128), f32),
            pltpu.VMEM((3, 128, 128), f32),
            pltpu.VMEM((4, 128, 128), f32),
            pltpu.VMEM((5, 8, 128), f32),
            pltpu.VMEM((4, 7, 48, 128), f32),
            pltpu.VMEM((4, 48, 128), f32),
            pltpu.VMEM((4, 8, 48, 128), f32),
            pltpu.VMEM((2, 8, 96, 128), f32),
            pltpu.VMEM((4, 4, 96, 128), f32),
            pltpu.VMEM((4, 4, 96, 128), f32),
            dma((8,)),
            dma((5,)), dma((5,)),
            dma((5, 2, 16)), dma((5, 2)),
            dma((5,)), dma((5,)),
            dma((5,)), dma((5,)),
            dma((4, 8)), dma((4, 8)),
            dma((4, 8)), dma((4, 8)),
            dma((5,)), dma((5,)),
            dma((4, 4)), dma((4, 4)),
            dma((4, 4)), dma((4, 4)),
            dma((16,)), dma((16,)),
        ],
        compiler_params=pltpu.CompilerParams(
            collective_id=0, has_side_effects=True, vmem_limit_bytes=48 * 1024 * 1024
        ),
        name="whiten",
    )(jacobian.T, factor_cols, diag_inverse)
    return jnp.transpose(out, (0, 2, 1)).reshape(2048, 192)


def solution(mesh):
    in_specs = (P("rows", None), P(None, "cols", "rows"), P(None, "cols", None))
    return jax.shard_map(
        per_device, mesh=mesh, in_specs=in_specs, out_specs=P("rows", None), check_vma=False
    )
```

time: 121 us -> 105 us (0.87)
  Pallas kernels: 118 us -> 101 us
    pallas_call x1, Pallas kernels: 118 us -> 101 us  [per_device(): pl.pallas_call(kernel, out_shape=jax.ShapeDtypeStruct((16, 192, 128), f32...]
    unnamed x3 -> x4, local copies, waits for them, and re-layouts: 1.94 us -> 2.72 us
where the time goes in v2:
time: 105 us
  Pallas kernels  101 us (96%)
  local copies, waits for them, and re-layouts  4.05 us (4%)
    pallas_call x1, Pallas kernels, per_device(): pl.pallas_call(kernel, out_shape=jax.ShapeDtypeStruct((16, 192, 128), f32...  101 us
    unnamed x4, local copies, waits for them, and re-layouts  2.72 us

profile of v2, /device:TPU:1, one launch (start us, length us, event | category | flops | bytes accessed | tf_op | source)
XLA Modules:
  0.0 105.3 jit_solution(10910121705871149822)
XLA Ops:
  0.0 0.0 copy-start
  0.0 1.4 %copy-done = f32[2048,192]{0,1:T(8,128)S(1)} copy-done((f32[2048,192]{0,1:T(8,128)S(1)}, f32[2048,192]{0,1:T(8,128)}, u32[]{:S(2)}) %copy-start) | copy-done | bytes 1572888
  1.4 0.0 copy-start.1
  1.4 1.3 %copy-done.1 = f32[5,64,1024]{2,1,0:T(8,128)S(1)} copy-done((f32[5,64,1024]{2,1,0:T(8,128)S(1)}, f32[5,64,1024]{2,1,0:T(8,128)}, u32[]{:S(2)}) %copy-start.1) | copy-done | bytes 1310744
  2.7 101.2 %whiten.1 = f32[16,192,128]{2,1,0:T(8,128)S(1)} custom-call(f32[192,2048]{1,0:T(8,128)S(1)} %bitcast.7, f32[5,64,2048]{2,1,0:T(8,128)} %fac.1, f32[5,64,1024]{2,1,0:T(8,128)S(1)} %copy-done.1), custom_call_target="tpu_custom_call" | custom-call | tf_op jit(solution)/shard_map/whiten/pallas_call | solution.py:433
  103.9 1.3 %copy_bitcast_fusion = f32[2048,192]{0,1:T(8,128)} fusion(f32[16,192,128]{2,1,0:T(8,128)S(1)} %whiten.1), kind=kLoop, calls=%fused_computation | loop fusion | bytes 3145728 | tf_op jit(solution)/shard_map/reshape | solution.py:475
Async XLA Ops:
  0.0 1.4 %copy-start = (f32[2048,192]{0,1:T(8,128)S(1)}, f32[2048,192]{0,1:T(8,128)}, u32[]{:S(2)}) copy-start(f32[2048,192]{0,1:T(8,128)} %param.3) | copy-start | bytes 4718596
  1.4 1.3 %copy-start.1 = (f32[5,64,1024]{2,1,0:T(8,128)S(1)}, f32[5,64,1024]{2,1,0:T(8,128)}, u32[]{:S(2)}) copy-start(f32[5,64,1024]{2,1,0:T(8,128)} %dinv.1) | copy-start | bytes 3932164

commit v3 on v2

--- a/solution.py
+++ b/solution.py
@@ -37,8 +37,8 @@
 
 def kernel(
     jac, fac, dinv, out,
-    dv, fv, jt, js, x0, t1, ts, tp, xf, lt2, lt3, lt4, jtile,
-    pa, ss, sb, u, rsend, rbuf,
+    dv, fv, jt, js, x0, t1, tpart, tin, stage_f, ts, tp, xf, lt2, lt3, lt4, jtile,
+    pa, ss, sb, u, rsend, rbuf, og,
     load_sem, pair_send, pair_recv, own_send, own_recv, fwd_send, fwd_recv, pass_send, pass_recv,
     a_send, a_recv, b_send, b_recv, h_send, h_recv, r_send, r_recv, g_send, g_recv, o_send, o_recv,
 ):
@@ -67,6 +67,13 @@
 
     sent = []
 
+    bar = pltpu.get_barrier_semaphore()
+    for d in range(1, 16):
+        pl.semaphore_signal(bar, inc=1, device_id=rdev(d), device_id_type=MESH)
+    for d in range(1, 8):
+        pl.semaphore_signal(bar, inc=1, device_id=zdev(d), device_id_type=MESH)
+    pl.semaphore_signal(bar, inc=1, device_id=partner, device_id_type=MESH)
+
     mine = subl(core, 64)
     first_rows = pl.ds(1024, 1024)
     load_0 = [
@@ -87,19 +94,109 @@
     for cp in load_j:
         cp.start()
 
-    load_jt = pltpu.make_async_copy(jac.at[subl(core, 96), :], jt, load_sem.at[4])
+    load_jt = pltpu.make_async_copy(jac, jt, load_sem.at[4])
 
     @pl.when(r == 0)
     def _():
         load_jt.start()
-
-    bar = pltpu.get_barrier_semaphore()
-    for d in range(1, 16):
-        pl.semaphore_signal(bar, inc=1, device_id=rdev(d), device_id_type=MESH)
-    for d in range(1, 8):
-        pl.semaphore_signal(bar, inc=1, device_id=zdev(d), device_id_type=MESH)
-    pl.semaphore_signal(bar, inc=1, device_id=partner, device_id_type=MESH)
+        for cp in load_0:
+            cp.wait()
+        load_jt.wait()
+        first = dot3(jt[:, 0:1024], dv[0, mine, :], NT)
+        whole = dot3(first, fv[0, mine, 1024:2048], NN)
+        for i in range(8):
+            for k in range(2):
+                tpart[k, i] = whole[k * 96:(k + 1) * 96, i * 128:(i + 1) * 128]
+
+        @pl.when(c == 0)
+        def _():
+            for i in range(8):
+                for k in range(2):
+                    tpart[k, i] = tpart[k, i] - jt[k * 96:(k + 1) * 96, 1024 + i * 128:1024 + (i + 1) * 128]
+
+    lts = {2: lt2, 3: lt3, 4: lt4}
+    owner_h = {2: 0, 3: 0, 4: 1}
+
+    def fac_copy(j, k, fetch=False):
+        tx = (x + k // 2) % 4
+        ty = h * 2 + (y % 2 + k % 2) % 2
+        tg = tx * 2 + (ty + h) % 2
+        rows = pl.ds(pl.multiple_of((j % 2) * 1024 + tg * 128, 128), 128)
+        dst = lts[j].at[:, mine, :]
+        part = stage_f.at[pl.ds(0 if j == 4 else 3 * (j - 2), j), k]
+        if fetch:
+            return pltpu.make_async_copy(fac.at[pl.ds(0, j), :, rows], dst if k == 0 else part, own_send.at[j, 0, k] if k else own_recv.at[j, 0])
+        return remote(part, dst, own_send.at[j, 0, k], own_recv.at[j, 0], {"rows": tx * 4 + ty})
+
+    def jac_copy(j, d):
+        to = (r + d) % 16
+        tx = to // 4
+        ty = to % 4
+        th = ty // 2
+        tg = tx * 2 + (ty + th) % 2
+        rows = pl.ds(pl.multiple_of((j % 2) * 1024 + tg * 128, 128), 128)
+        src = jac.at[pl.ds(pl.multiple_of(core * 96 + th * 48 + z * 8, 8), 8), rows]
+        if d == 0:
+            return pltpu.make_async_copy(src, jtile.at[j], own_recv.at[j, 1])
+        return remote(src, jtile.at[j], own_send.at[j, 1, d], own_recv.at[j, 1], rdev(d))
+
+    def fetch_fac(j):
+        for k in (4, 5, 2, 3, 6, 7, 1, 0):
+            fac_copy(j, k, True).start()
+
+    def send_fac(j):
+        for k in (4, 5, 2, 3, 6, 7, 1):
+            fac_copy(j, k, True).wait()
+            fac_copy(j, k).start()
+
+    def send_jac(j):
+        @pl.when(z < 6)
+        def _():
+            for d in range(16):
+                jac_copy(j, d).start()
+
+    def wait_fac(j):
+        @pl.when(h == owner_h[j])
+        def _():
+            pltpu.make_async_copy(lts[j].at[:, mine, :], lts[j].at[:, mine, :], own_recv.at[j, 0]).wait()
+            fac_pass(j).start()
+
+        @pl.when(h != owner_h[j])
+        def _():
+            fac_pass(j).wait_recv()
+
+    def fac_pass(j):
+        return remote(lts[j].at[:, mine, :], lts[j].at[:, mine, :], pass_send.at[j], pass_recv.at[j], hdev)
+
+    def wait_jac(j):
+        @pl.when(z < 6)
+        def _():
+            pltpu.make_async_copy(jtile.at[j], jtile.at[j], own_recv.at[j, 1]).wait()
+
+    def wait_owner_sends(j):
+        for k in range(1, 8):
+            fac_copy(j, k).wait_send()
+
+        @pl.when(z < 6)
+        def _():
+            for d in range(1, 16):
+                jac_copy(j, d).wait_send()
+
+    @pl.when(r == 1)
+    def _():
+        fetch_fac(2)
+        fetch_fac(3)
+
+    @pl.when(r == 2)
+    def _():
+        fetch_fac(4)
+
     pl.semaphore_wait(bar, 23)
+    swap_t = remote(tpart.at[1 - core], tin, pair_send.at[5], pair_recv.at[5], partner)
+
+    @pl.when(r == 0)
+    def _():
+        swap_t.start()
 
     pair = [
         remote(src, dst, pair_send.at[i], pair_recv.at[i], partner)
@@ -117,68 +214,6 @@
         cp.start()
         sent.append(cp)
 
-    lts = {2: lt2, 3: lt3, 4: lt4}
-    owner_h = {2: 0, 3: 0, 4: 1}
-
-    def fac_copy(j, k):
-        tx = (x + k // 2) % 4
-        ty = h * 2 + (y % 2 + k % 2) % 2
-        tg = tx * 2 + (ty + h) % 2
-        rows = pl.ds(pl.multiple_of((j % 2) * 1024 + tg * 128, 128), 128)
-        src, dst = fac.at[pl.ds(0, j), :, rows], lts[j].at[:, mine, :]
-        if k == 0:
-            return pltpu.make_async_copy(src, dst, own_recv.at[j, 0])
-        return remote(src, dst, own_send.at[j, 0, k], own_recv.at[j, 0], {"rows": tx * 4 + ty})
-
-    def jac_copy(j, d):
-        to = (r + d) % 16
-        tx = to // 4
-        ty = to % 4
-        th = ty // 2
-        tg = tx * 2 + (ty + th) % 2
-        rows = pl.ds(pl.multiple_of((j % 2) * 1024 + tg * 128, 128), 128)
-        src = jac.at[pl.ds(pl.multiple_of(core * 96 + th * 48 + z * 8, 8), 8), rows]
-        if d == 0:
-            return pltpu.make_async_copy(src, jtile.at[j], own_recv.at[j, 1])
-        return remote(src, jtile.at[j], own_send.at[j, 1, d], own_recv.at[j, 1], rdev(d))
-
-    def send_fac(j):
-        for k in (4, 5, 2, 3, 6, 7, 1, 0):
-            fac_copy(j, k).start()
-
-    def send_jac(j):
-        @pl.when(z < 6)
-        def _():
-            for d in range(16):
-                jac_copy(j, d).start()
-
-    def wait_fac(j):
-        @pl.when(h == owner_h[j])
-        def _():
-            pltpu.make_async_copy(lts[j].at[:, mine, :], lts[j].at[:, mine, :], own_recv.at[j, 0]).wait()
-            fac_pass(j).start()
-
-        @pl.when(h != owner_h[j])
-        def _():
-            fac_pass(j).wait_recv()
-
-    def fac_pass(j):
-        return remote(lts[j].at[:, mine, :], lts[j].at[:, mine, :], pass_send.at[j], pass_recv.at[j], hdev)
-
-    def wait_jac(j):
-        @pl.when(z < 6)
-        def _():
-            pltpu.make_async_copy(jtile.at[j], jtile.at[j], own_recv.at[j, 1]).wait()
-
-    def wait_owner_sends(j):
-        for k in range(1, 8):
-            fac_copy(j, k).wait_send()
-
-        @pl.when(z < 6)
-        def _():
-            for d in range(1, 16):
-                jac_copy(j, d).wait_send()
-
     @pl.when(r == 1)
     def _():
         send_fac(2)
@@ -191,10 +226,10 @@
         send_fac(4)
         send_jac(4)
 
-    for cp in load_0:
-        cp.wait()
-    for cp in pair[:2]:
-        cp.wait_recv()
+    @pl.when(r != 0)
+    def _():
+        for cp in load_0:
+            cp.wait()
 
     half = subl(core, 96)
     quarter = subl(h, 48)
@@ -212,24 +247,21 @@
 
     @pl.when(r == 0)
     def _():
-        load_jt.wait()
-        first = dot3(jt[:, 0:1024], dv[0], NT)
-        x0[...] = first
-        whole = dot3(first, fv[0, :, 1024:2048], NN)
+        swap_t.wait_recv()
         for i in range(8):
-            t1[i] = whole[:, i * 128:(i + 1) * 128]
-
-        @pl.when(z == 0)
-        def _():
-            for i in range(8):
-                t1[i] = t1[i] - jt[:, 1024 + i * 128:1024 + (i + 1) * 128]
-
+            t1[i] = tpart[core, i] + tin[i]
         for d in FAR:
             first_copy(d)[0].start()
+        ts[1] = t1[0, 0:48]
+        pair[0].wait_recv()
+        x0[...] = dot3(jt[half, 0:1024], dv[0], NT)
         for d in FAR:
             first_copy(d)[1].start()
-        ts[1] = t1[0, 0:48]
         xf[0, 0:48] = x0[0:48]
+
+    @pl.when(r != 0)
+    def _():
+        pair[0].wait_recv()
 
     for cp in pair[2:]:
         cp.start()
@@ -264,7 +296,7 @@
         if j == 0:
             for cp in (load_f, load_g):
                 cp.wait()
-            for cp in pair[3:]:
+            for cp in (pair[1], pair[3], pair[4]):
                 cp.wait_recv()
         for b in range(2):
             part = dot3(xf[j], fv[j, :, b * 1024:(b + 1) * 1024], NN)
@@ -356,16 +388,9 @@
             got[i] = cp
 
     def piece(b, origin):
-        return out.at[b * 8 + origin, half]
+        return og.at[b * 8 + origin]
 
     gather = {}
-    last = []
-
-    def share(b, origin, k):
-        cp = remote(piece(b, origin), piece(b, origin), o_send.at[k], o_recv.at[k], partner)
-        cp.start()
-        sent.append(cp)
-        last.append(cp)
 
     def hop(i, s):
         b, way, hops = gpaths[i]
@@ -385,12 +410,10 @@
         block = r * 2 + b
         solved = xf[jnp.minimum(block, 4)]
         updated = js[b] - total
-        out[b * 8 + z, half] = jnp.where(block < 5, solved, updated)
+        og[b * 8 + z] = jnp.where(block < 5, solved, updated)
         for i in range(4):
             if gpaths[i][0] == b:
                 hop(i, 0)
-        share(b, z, b)
-    k = 2
     for s in range(1, 5):
         for i in range(4):
             b, way, hops = gpaths[i]
@@ -399,15 +422,19 @@
             gather[i].wait_recv()
             if s < hops:
                 hop(i, s)
-            share(b, (z - way * s + 8) % 8, k)
-            k += 1
-    for cp in last:
-        cp.wait_recv()
+    last = remote(og, out.at[:, half], o_send, o_recv, partner)
+    last.start()
+    sent.append(last)
+    keep = pltpu.make_async_copy(og, out.at[:, half], load_sem.at[8])
+    keep.start()
+    keep.wait()
+    last.wait_recv()
     for cp in sent:
         cp.wait_send()
 
     @pl.when(r == 0)
     def _():
+        swap_t.wait_send()
         for d in range(1, 16):
             for cp in first_copy(d):
                 cp.wait_send()
@@ -433,15 +460,18 @@
     out = pl.pallas_call(
         kernel,
         out_shape=jax.ShapeDtypeStruct((16, 192, 128), f32),
-        in_specs=[pl.BlockSpec(memory_space=pl.ANY)] * 3,
-        out_specs=pl.BlockSpec(memory_space=pltpu.VMEM),
+        in_specs=[pl.BlockSpec(memory_space=pltpu.HBM)] * 3,
+        out_specs=pl.BlockSpec(memory_space=pltpu.HBM),
         scratch_shapes=[
             pltpu.VMEM((5, 128, 1024), f32),
             pltpu.VMEM((5, 128, 2048), f32),
-            pltpu.VMEM((96, 2048), f32),
+            pltpu.VMEM((192, 2048), f32),
             pltpu.VMEM((2, 96, 128), f32),
             pltpu.VMEM((96, 128), f32),
             pltpu.VMEM((8, 96, 128), f32),
+            pltpu.VMEM((2, 8, 96, 128), f32),
+            pltpu.VMEM((8, 96, 128), f32),
+            pltpu.VMEM((6, 8, 64, 128), f32),
             pltpu.VMEM((5, 48, 128), f32),
             pltpu.VMEM((48, 128), f32),
             pltpu.VMEM((5, 96, 128), f32),
@@ -455,8 +485,9 @@
             pltpu.VMEM((2, 8, 96, 128), f32),
             pltpu.VMEM((4, 4, 96, 128), f32),
             pltpu.VMEM((4, 4, 96, 128), f32),
-            dma((8,)),
-            dma((5,)), dma((5,)),
+            pltpu.VMEM((16, 96, 128), f32),
+            dma((9,)),
+            dma((6,)), dma((6,)),
             dma((5, 2, 16)), dma((5, 2)),
             dma((5,)), dma((5,)),
             dma((5,)), dma((5,)),
@@ -465,10 +496,10 @@
             dma((5,)), dma((5,)),
             dma((4, 4)), dma((4, 4)),
             dma((4, 4)), dma((4, 4)),
-            dma((16,)), dma((16,)),
+            dma(()), dma(()),
         ],
         compiler_params=pltpu.CompilerParams(
-            collective_id=0, has_side_effects=True, vmem_limit_bytes=48 * 1024 * 1024
+            collective_id=0, has_side_effects=True, vmem_limit_bytes=57 * 1024 * 1024
         ),
         name="whiten",
     )(jacobian.T, factor_cols, diag_inverse)

time: 105 us -> 104 us (level)
  local copies, waits for them, and re-layouts: 4.05 us -> 2.73 us
    unnamed x4 -> x0, local copies, waits for them, and re-layouts: 2.72 us -> none
    reshape x1, local copies, waits for them, and re-layouts: 1.32 us -> 2.73 us  [per_device(): return jnp.transpose(out, (0, 2, 1)).reshape(2048, 192)]
where the time goes in v3:
time: 104 us
  Pallas kernels  101 us (97%)
  local copies, waits for them, and re-layouts  2.73 us (3%)
    pallas_call x1, Pallas kernels, per_device(): pl.pallas_call(kernel, out_shape=jax.ShapeDtypeStruct((16, 192, 128), f32...  101 us
    reshape x1, local copies, waits for them, and re-layouts, per_device(): return jnp.transpose(out, (0, 2, 1)).reshape(2048, 192)  2.73 us

profile of v3, /device:TPU:1, one launch (start us, length us, event | category | flops | bytes accessed | tf_op | source)
XLA Modules:
  0.0 103.9 jit_solution(241974674630342243)
XLA Ops:
  0.0 101.1 %whiten.1 = f32[16,192,128]{2,1,0:T(8,128)} custom-call(f32[192,2048]{1,0:T(8,128)} %bitcast.7, f32[5,64,2048]{2,1,0:T(8,128)} %fac.1, f32[5,64,1024]{2,1,0:T(8,128)} %dinv.1), custom_call_target="tpu_custom_call" | custom-call | tf_op jit(solution)/shard_map/whiten/pallas_call | solution.py:460
  101.1 2.7 %copy_bitcast_fusion = f32[2048,192]{0,1:T(8,128)} fusion(f32[16,192,128]{2,1,0:T(8,128)} %whiten.1), kind=kLoop, calls=%fused_computation | loop fusion | bytes 3145728 | tf_op jit(solution)/shard_map/reshape | solution.py:506

commit v4 on v3

--- a/solution.py
+++ b/solution.py
@@ -38,9 +38,9 @@
 def kernel(
     jac, fac, dinv, out,
     dv, fv, jt, js, x0, t1, tpart, tin, stage_f, ts, tp, xf, lt2, lt3, lt4, jtile,
-    pa, ss, sb, u, rsend, rbuf, og,
+    pa, ss, sb, u, rsend, rbuf, og, g4, xz,
     load_sem, pair_send, pair_recv, own_send, own_recv, fwd_send, fwd_recv, pass_send, pass_recv,
-    a_send, a_recv, b_send, b_recv, h_send, h_recv, r_send, r_recv, g_send, g_recv, o_send, o_recv,
+    a_send, a_recv, b_send, b_recv, h_send, h_recv, r_send, r_recv, g_send, g_recv, o_send, o_recv, z_send, z_recv, x_send, x_recv,
 ):
     r = lax.axis_index("rows")
     c = lax.axis_index("cols")
@@ -81,7 +81,7 @@
         pltpu.make_async_copy(fac.at[0, :, first_rows], fv.at[0, mine, first_rows], load_sem.at[1]),
     ]
     load_d = pltpu.make_async_copy(dinv.at[pl.ds(1, 4)], dv.at[pl.ds(1, 4), mine, :], load_sem.at[5])
-    load_f = pltpu.make_async_copy(fac.at[pl.ds(1, 4)], fv.at[pl.ds(1, 4), mine, :], load_sem.at[6])
+    load_f = pltpu.make_async_copy(fac.at[pl.ds(1, 3)], fv.at[pl.ds(1, 3), mine, :], load_sem.at[6])
     load_g = pltpu.make_async_copy(fac.at[0, :, pl.ds(0, 1024)], fv.at[0, mine, pl.ds(0, 1024)], load_sem.at[7])
     for cp in load_0:
         cp.start()
@@ -205,7 +205,7 @@
                 (dinv.at[0], dv.at[0, mine, :]),
                 (fac.at[0, :, first_rows], fv.at[0, mine, first_rows]),
                 (dinv.at[pl.ds(1, 4)], dv.at[pl.ds(1, 4), mine, :]),
-                (fac.at[pl.ds(1, 4)], fv.at[pl.ds(1, 4), mine, :]),
+                (fac.at[pl.ds(1, 3)], fv.at[pl.ds(1, 3), mine, :]),
                 (fac.at[0, :, pl.ds(0, 1024)], fv.at[0, mine, pl.ds(0, 1024)]),
             )
         )
@@ -268,6 +268,20 @@
         sent.append(cp)
     for cp in (load_d, load_f, load_g):
         cp.start()
+    def spread_copy(d, b):
+        rows = lanes(b * 8 + (z + d) % 8)
+        if d == 0:
+            return pltpu.make_async_copy(fac.at[4, :, rows], g4.at[core, z, b], z_recv.at[0, b])
+        return remote(fac.at[4, :, rows], g4.at[core, z, b], z_send.at[d, b], z_recv.at[d, b], zdev(d))
+
+    def start_spread():
+        @pl.when(r >= 2)
+        def _():
+            for d in (4, 3, 5, 2, 6, 1, 7, 0):
+                for b in range(2):
+                    spread_copy(d, b).start()
+
+    start_spread()
     for cp in load_j:
         cp.wait()
 
@@ -284,6 +298,40 @@
 
     fwd = {}
     swap = {}
+
+    def spread_pair():
+        return remote(g4.at[core], g4.at[core], z_send.at[0, 0], z_recv.at[8, 0], partner)
+
+    def spread_on():
+        @pl.when(r >= 2)
+        def _():
+            for d in range(8):
+                for b in range(2):
+                    if d:
+                        spread_copy(d, b).wait_recv()
+                    else:
+                        spread_copy(d, b).wait()
+            spread_pair().start()
+
+    paths = ((0, -1, 4), (1, 1, 4), (0, 1, 3), (1, -1, 3))
+
+    def ring_copy(i, s):
+        b, way, hops = paths[i]
+        return remote(rsend.at[i, s], rbuf.at[i, s], r_send.at[i, s], r_recv.at[i, s], zdev(way))
+
+    def ring(s):
+        @pl.when(r >= 2)
+        def _():
+            for i, (b, way, hops) in enumerate(paths):
+                if s >= hops:
+                    continue
+                target = (z + way * (hops - s) + 8) % 8
+                value = u[b, target]
+                if s > 0:
+                    ring_copy(i, s - 1).wait_recv()
+                    value = value + rbuf[i, s - 1]
+                rsend[i, s] = value
+                ring_copy(i, s).start()
 
     def exchange(j):
         cp = remote(xf.at[j, quarter, :], xf.at[j, quarter, :], h_send.at[j], h_recv.at[j], hdev)
@@ -324,6 +372,10 @@
             update(0)
         if j > 1:
             update(j - 1)
+        if j == 3:
+            spread_on()
+        if j == 4:
+            ring(0)
         for cp in stage:
             cp.wait_recv()
         total = ts[j]
@@ -346,6 +398,8 @@
         sent.extend(stage)
         if j == 1:
             fwd[3] = forward(3)
+        if j == 4:
+            ring(1)
         if j < 4:
             fwd[j + 1].wait_recv()
             part = dot3(xf[0, quarter, :], lts[j + 1][0], NN)
@@ -358,6 +412,8 @@
         for cp in stage:
             cp.wait_recv()
         new = dot3(jnp.concatenate([sb[j - 1, i] for i in range(8)], axis=1), dv[j], NT)
+        if j == 4:
+            break
         xf[j, quarter, :] = new
         if j < 4:
             ts[j + 1] = tp[...] + dot3(new, lts[j + 1][j], NN)
@@ -368,24 +424,39 @@
                 ts[j + 1, subl(z, 8)] = ts[j + 1, subl(z, 8)] - jtile[j + 1]
         exchange(j)
 
-    update(4)
-
-    paths = ((0, -1, 4), (1, 1, 4), (0, 1, 3), (1, -1, 3))
-    got = [None] * 4
-    for s in range(4):
-        for i, (b, way, hops) in enumerate(paths):
-            if s >= hops:
-                continue
-            target = (z + way * (hops - s) + 8) % 8
-            value = u[b, target]
-            if s > 0:
-                got[i].wait_recv()
-                value = value + rbuf[i, s - 1]
-            rsend[i, s] = value
-            cp = remote(rsend.at[i, s], rbuf.at[i, s], r_send.at[i, s], r_recv.at[i, s], zdev(way))
-            cp.start()
-            sent.append(cp)
-            got[i] = cp
+    xz[h, z] = new
+
+    def pass_on(i, k):
+        cp = remote(xz.at[h, i], xz.at[h, i], x_send.at[k], x_recv.at[k], hdev)
+        cp.start()
+        sent.append(cp)
+        return cp
+
+    stage = {}
+    for d in (4, 3, 5, 2, 6, 1, 7):
+        cp = remote(xz.at[h, z], xz.at[h, z], x_send.at[8 + d], x_recv.at[8 + d], zdev(d))
+        cp.start()
+        sent.append(cp)
+        stage[d] = cp
+    passed = [pass_on(z, 0)]
+    ring(2)
+    for d in (1, 7, 2, 6, 3, 5, 4):
+        stage[d].wait_recv()
+        passed.append(pass_on((z - d + 8) % 8, d))
+    ring(3)
+
+    @pl.when(r >= 2)
+    def _():
+        spread_pair().wait_recv()
+
+    for cp in passed:
+        cp.wait_recv()
+    xf[4] = jnp.concatenate([xz[0, z], xz[1, z]], axis=0)
+    left = jnp.concatenate([jnp.concatenate([xz[k, i] for i in range(8)], axis=1) for k in range(2)], axis=0)
+    right = jnp.concatenate(
+        [jnp.concatenate([g4[k, i, b] for i in range(8) for k in range(2)], axis=0) for b in range(2)], axis=1
+    )
+    tail = dot3(left, right, NN)
 
     def piece(b, origin):
         return og.at[b * 8 + origin]
@@ -401,12 +472,15 @@
         gather[i] = cp
 
     gpaths = ((0, 1, 4), (1, -1, 4), (0, -1, 3), (1, 1, 3))
+
+    @pl.when(r >= 2)
+    def _():
+        for i, (b, way, hops) in enumerate(paths):
+            ring_copy(i, hops - 1).wait_recv()
+
     for b in range(2):
-        for i, (pb, way, hops) in enumerate(paths):
-            if pb == b:
-                got[i].wait_recv()
         first, second = [i for i in range(4) if paths[i][0] == b]
-        total = u[b, z] + rbuf[first, paths[first][2] - 1] + rbuf[second, paths[second][2] - 1]
+        total = tail[:, b * 128:(b + 1) * 128] + u[b, z] + rbuf[first, paths[first][2] - 1] + rbuf[second, paths[second][2] - 1]
         block = r * 2 + b
         solved = xf[jnp.minimum(block, 4)]
         updated = js[b] - total
@@ -414,6 +488,19 @@
         for i in range(4):
             if gpaths[i][0] == b:
                 hop(i, 0)
+    done = [(0, z), (1, z)]
+    shared = []
+
+    def share():
+        while done:
+            b, origin = done.pop()
+            p = b * 8 + origin
+            k = len(shared)
+            cp = remote(og.at[p], out.at[p, half], o_send.at[k], o_recv.at[k], partner)
+            cp.start()
+            sent.append(cp)
+            shared.append(cp)
+
     for s in range(1, 5):
         for i in range(4):
             b, way, hops = gpaths[i]
@@ -422,15 +509,26 @@
             gather[i].wait_recv()
             if s < hops:
                 hop(i, s)
-    last = remote(og, out.at[:, half], o_send, o_recv, partner)
-    last.start()
-    sent.append(last)
+            done.append((b, (z - way * s + 8) % 8))
+        if s >= 3:
+            share()
     keep = pltpu.make_async_copy(og, out.at[:, half], load_sem.at[8])
     keep.start()
     keep.wait()
-    last.wait_recv()
+    for cp in shared:
+        cp.wait_recv()
     for cp in sent:
         cp.wait_send()
+
+    @pl.when(r >= 2)
+    def _():
+        for d in range(1, 8):
+            for b in range(2):
+                spread_copy(d, b).wait_send()
+        spread_pair().wait_send()
+        for i, (b, way, hops) in enumerate(paths):
+            for s in range(hops):
+                ring_copy(i, s).wait_send()
 
     @pl.when(r == 0)
     def _():
@@ -464,7 +562,7 @@
         out_specs=pl.BlockSpec(memory_space=pltpu.HBM),
         scratch_shapes=[
             pltpu.VMEM((5, 128, 1024), f32),
-            pltpu.VMEM((5, 128, 2048), f32),
+            pltpu.VMEM((4, 128, 2048), f32),
             pltpu.VMEM((192, 2048), f32),
             pltpu.VMEM((2, 96, 128), f32),
             pltpu.VMEM((96, 128), f32),
@@ -486,6 +584,8 @@
             pltpu.VMEM((4, 4, 96, 128), f32),
             pltpu.VMEM((4, 4, 96, 128), f32),
             pltpu.VMEM((16, 96, 128), f32),
+            pltpu.VMEM((2, 8, 2, 64, 128), f32),
+            pltpu.VMEM((2, 8, 48, 128), f32),
             dma((9,)),
             dma((6,)), dma((6,)),
             dma((5, 2, 16)), dma((5, 2)),
@@ -496,7 +596,9 @@
             dma((5,)), dma((5,)),
             dma((4, 4)), dma((4, 4)),
             dma((4, 4)), dma((4, 4)),
-            dma(()), dma(()),
+            dma((16,)), dma((16,)),
+            dma((8, 2)), dma((9, 2)),
+            dma((16,)), dma((16,)),
         ],
         compiler_params=pltpu.CompilerParams(
             collective_id=0, has_side_effects=True, vmem_limit_bytes=57 * 1024 * 1024

time: 104 us -> 102 us (0.981)
  Pallas kernels: 101 us -> 99.1 us
    pallas_call x1, Pallas kernels: 101 us -> 99.1 us  [per_device(): pl.pallas_call(kernel, out_shape=jax.ShapeDtypeStruct((16, 192, 128), f32...]
where the time goes in v4:
time: 102 us
  Pallas kernels  99.1 us (97%)
  local copies, waits for them, and re-layouts  2.73 us (3%)
    pallas_call x1, Pallas kernels, per_device(): pl.pallas_call(kernel, out_shape=jax.ShapeDtypeStruct((16, 192, 128), f32...  99.1 us
    reshape x1, local copies, waits for them, and re-layouts, per_device(): return jnp.transpose(out, (0, 2, 1)).reshape(2048, 192)  2.73 us

profile of v4, /device:TPU:1, one launch (start us, length us, event | category | flops | bytes accessed | tf_op | source)
XLA Modules:
  0.0 101.9 jit_solution(15476560607750550503)
XLA Ops:
  0.0 99.1 %whiten.1 = f32[16,192,128]{2,1,0:T(8,128)} custom-call(f32[192,2048]{1,0:T(8,128)} %bitcast.7, f32[5,64,2048]{2,1,0:T(8,128)} %fac.1, f32[5,64,1024]{2,1,0:T(8,128)} %dinv.1), custom_call_target="tpu_custom_call" | custom-call | tf_op jit(solution)/shard_map/whiten/pallas_call | solution.py:558
  99.1 2.7 %copy_bitcast_fusion = f32[2048,192]{0,1:T(8,128)} fusion(f32[16,192,128]{2,1,0:T(8,128)} %whiten.1), kind=kLoop, calls=%fused_computation | loop fusion | bytes 3145728 | tf_op jit(solution)/shard_map/reshape | solution.py:608

commit v5 on v4

--- a/solution.py
+++ b/solution.py
@@ -27,6 +27,15 @@
     return one(ah, bh) + (one(ah, bl) + one(al, bh))
 
 
+def dot3_split(a, bh, bl, dims):
+    ah, al = halves(a)
+
+    def one(p, q):
+        return lax.dot_general(p, q, dims, preferred_element_type=jnp.float32)
+
+    return one(ah, bh) + (one(ah, bl) + one(al, bh))
+
+
 def lanes(i, n=128):
     return pl.ds(pl.multiple_of(i * n, n), n)
 
@@ -38,7 +47,7 @@
 def kernel(
     jac, fac, dinv, out,
     dv, fv, jt, js, x0, t1, tpart, tin, stage_f, ts, tp, xf, lt2, lt3, lt4, jtile,
-    pa, ss, sb, u, rsend, rbuf, og, g4, xz,
+    pa, ss, sb, u, rsend, rbuf, og, g4, xz, dsplit,
     load_sem, pair_send, pair_recv, own_send, own_recv, fwd_send, fwd_recv, pass_send, pass_recv,
     a_send, a_recv, b_send, b_recv, h_send, h_recv, r_send, r_recv, g_send, g_recv, o_send, o_recv, z_send, z_recv, x_send, x_recv,
 ):
@@ -210,9 +219,10 @@
             )
         )
     ]
-    for cp in pair[:2]:
-        cp.start()
-        sent.append(cp)
+
+    @pl.when(r == 0)
+    def _():
+        pair[0].start()
 
     @pl.when(r == 1)
     def _():
@@ -259,15 +269,6 @@
             first_copy(d)[1].start()
         xf[0, 0:48] = x0[0:48]
 
-    @pl.when(r != 0)
-    def _():
-        pair[0].wait_recv()
-
-    for cp in pair[2:]:
-        cp.start()
-        sent.append(cp)
-    for cp in (load_d, load_f, load_g):
-        cp.start()
     def spread_copy(d, b):
         rows = lanes(b * 8 + (z + d) % 8)
         if d == 0:
@@ -282,6 +283,9 @@
                     spread_copy(d, b).start()
 
     start_spread()
+    pair[2].start()
+    sent.append(pair[2])
+    load_d.start()
     for cp in load_j:
         cp.wait()
 
@@ -360,6 +364,11 @@
             stage.append(cp)
         sent.extend(stage)
         if j == 1:
+            for cp in (pair[1], pair[3], pair[4]):
+                cp.start()
+                sent.append(cp)
+            load_f.start()
+            load_g.start()
             fwd[2] = forward(2)
 
             @pl.when(r != 0)
@@ -367,15 +376,19 @@
                 pltpu.make_async_copy(xf.at[0, quarter], xf.at[0, quarter], own_recv.at[0, 1]).wait()
 
             exchange(0)
-        if j == 2:
-            fwd[4] = forward(4)
-            update(0)
-        if j > 1:
-            update(j - 1)
-        if j == 3:
+            load_d.wait()
+            pair[2].wait_recv()
+        elif j < 4:
+            fwd[j + 1] = forward(j + 1)
+            update(j - 2)
+        else:
+            update(2)
             spread_on()
-        if j == 4:
+            update(3)
             ring(0)
+        hi, lo = halves(dv[j])
+        dsplit[0] = hi
+        dsplit[1] = lo
         for cp in stage:
             cp.wait_recv()
         total = ts[j]
@@ -396,8 +409,6 @@
                 cp.start()
                 stage.append(cp)
         sent.extend(stage)
-        if j == 1:
-            fwd[3] = forward(3)
         if j == 4:
             ring(1)
         if j < 4:
@@ -406,12 +417,10 @@
             for m in range(1, j):
                 part = part + dot3(xf[m, quarter, :], lts[j + 1][m], NN)
             tp[...] = part
-        if j == 1:
-            load_d.wait()
-            pair[2].wait_recv()
         for cp in stage:
             cp.wait_recv()
-        new = dot3(jnp.concatenate([sb[j - 1, i] for i in range(8)], axis=1), dv[j], NT)
+        rows = jnp.concatenate([sb[j - 1, i] for i in range(8)], axis=1)
+        new = dot3_split(rows, dsplit[0], dsplit[1], NT)
         if j == 4:
             break
         xf[j, quarter, :] = new
@@ -449,14 +458,15 @@
     def _():
         spread_pair().wait_recv()
 
+    right = jnp.concatenate(
+        [jnp.concatenate([g4[k, i, b] for i in range(8) for k in range(2)], axis=0) for b in range(2)], axis=1
+    )
+    right_hi, right_lo = halves(right)
     for cp in passed:
         cp.wait_recv()
     xf[4] = jnp.concatenate([xz[0, z], xz[1, z]], axis=0)
     left = jnp.concatenate([jnp.concatenate([xz[k, i] for i in range(8)], axis=1) for k in range(2)], axis=0)
-    right = jnp.concatenate(
-        [jnp.concatenate([g4[k, i, b] for i in range(8) for k in range(2)], axis=0) for b in range(2)], axis=1
-    )
-    tail = dot3(left, right, NN)
+    tail = dot3_split(left, right_hi, right_lo, NN)
 
     def piece(b, origin):
         return og.at[b * 8 + origin]
@@ -533,6 +543,7 @@
     @pl.when(r == 0)
     def _():
         swap_t.wait_send()
+        pair[0].wait_send()
         for d in range(1, 16):
             for cp in first_copy(d):
                 cp.wait_send()
@@ -586,6 +597,7 @@
             pltpu.VMEM((16, 96, 128), f32),
             pltpu.VMEM((2, 8, 2, 64, 128), f32),
             pltpu.VMEM((2, 8, 48, 128), f32),
+            pltpu.VMEM((2, 128, 1024), jnp.bfloat16),
             dma((9,)),
             dma((6,)), dma((6,)),
             dma((5, 2, 16)), dma((5, 2)),

time: 102 us -> 99 us (0.971)
  Pallas kernels: 99.1 us -> 96.1 us
    pallas_call x1, Pallas kernels: 99.1 us -> 96.1 us  [per_device(): pl.pallas_call(kernel, out_shape=jax.ShapeDtypeStruct((16, 192, 128), f32...]
where the time goes in v5:
time: 99 us; the launch traced here: 98.8 us
  Pallas kernels  96.1 us (97%)
  local copies, waits for them, and re-layouts  2.73 us (3%)
    pallas_call x1, Pallas kernels, per_device(): pl.pallas_call(kernel, out_shape=jax.ShapeDtypeStruct((16, 192, 128), f32...  96.1 us
    reshape x1, local copies, waits for them, and re-layouts, per_device(): return jnp.transpose(out, (0, 2, 1)).reshape(2048, 192)  2.73 us

profile of v5, /device:TPU:1, one launch (start us, length us, event | category | flops | bytes accessed | tf_op | source)
XLA Modules:
  0.0 98.8 jit_solution(8935799290224930526)
XLA Ops:
  0.0 96.1 %whiten.1 = f32[16,192,128]{2,1,0:T(8,128)} custom-call(f32[192,2048]{1,0:T(8,128)} %bitcast.7, f32[5,64,2048]{2,1,0:T(8,128)} %fac.1, f32[5,64,1024]{2,1,0:T(8,128)} %dinv.1), custom_call_target="tpu_custom_call" | custom-call | tf_op jit(solution)/shard_map/whiten/pallas_call | solution.py:569
  96.1 2.7 %copy_bitcast_fusion = f32[2048,192]{0,1:T(8,128)} fusion(f32[16,192,128]{2,1,0:T(8,128)} %whiten.1), kind=kLoop, calls=%fused_computation | loop fusion | bytes 3145728 | tf_op jit(solution)/shard_map/reshape | solution.py:620

commit v6 on v5

--- a/solution.py
+++ b/solution.py
@@ -380,10 +380,13 @@
             pair[2].wait_recv()
         elif j < 4:
             fwd[j + 1] = forward(j + 1)
-            update(j - 2)
+            if j == 2:
+                update(0)
+                update(1)
+            else:
+                update(2)
+                spread_on()
         else:
-            update(2)
-            spread_on()
             update(3)
             ring(0)
         hi, lo = halves(dv[j])
@@ -473,15 +476,13 @@
 
     gather = {}
 
-    def hop(i, s):
-        b, way, hops = gpaths[i]
-        origin = (z - way * s + 8) % 8
-        cp = remote(piece(b, origin), piece(b, origin), g_send.at[i, s], g_recv.at[i, s], zdev(way))
+    def hop(b, k, origin, d):
+        cp = remote(piece(b, origin), piece(b, origin), g_send.at[b, k], g_recv.at[b, k], zdev(d))
         cp.start()
         sent.append(cp)
-        gather[i] = cp
-
-    gpaths = ((0, 1, 4), (1, -1, 4), (0, -1, 3), (1, 1, 3))
+        gather[b, k] = cp
+
+    ways = (1, -1)
 
     @pl.when(r >= 2)
     def _():
@@ -495,9 +496,9 @@
         solved = xf[jnp.minimum(block, 4)]
         updated = js[b] - total
         og[b * 8 + z] = jnp.where(block < 5, solved, updated)
-        for i in range(4):
-            if gpaths[i][0] == b:
-                hop(i, 0)
+        w = ways[b]
+        for k, d in enumerate((2 * w, -2 * w, w, -w)):
+            hop(b, k, z, d)
     done = [(0, z), (1, z)]
     shared = []
 
@@ -511,17 +512,30 @@
             sent.append(cp)
             shared.append(cp)
 
-    for s in range(1, 5):
-        for i in range(4):
-            b, way, hops = gpaths[i]
-            if s > hops:
-                continue
-            gather[i].wait_recv()
-            if s < hops:
-                hop(i, s)
-            done.append((b, (z - way * s + 8) % 8))
-        if s >= 3:
-            share()
+    def arrived(b, k, origin):
+        gather[b, k].wait_recv()
+        done.append((b, (origin + 16) % 8))
+
+    for b in range(2):
+        w = ways[b]
+        arrived(b, 0, z - 2 * w)
+        hop(b, 4, (z - 2 * w + 8) % 8, 2 * w)
+        hop(b, 5, (z - 2 * w + 8) % 8, w)
+    for b in range(2):
+        w = ways[b]
+        arrived(b, 1, z + 2 * w)
+        hop(b, 6, (z + 2 * w + 8) % 8, -w)
+    for b in range(2):
+        w = ways[b]
+        arrived(b, 2, z - w)
+        arrived(b, 3, z + w)
+    share()
+    for b in range(2):
+        w = ways[b]
+        arrived(b, 6, z + 3 * w)
+        arrived(b, 5, z - 3 * w)
+        arrived(b, 4, z - 4 * w)
+    share()
     keep = pltpu.make_async_copy(og, out.at[:, half], load_sem.at[8])
     keep.start()
     keep.wait()
@@ -607,7 +621,7 @@
             dma((4, 8)), dma((4, 8)),
             dma((5,)), dma((5,)),
             dma((4, 4)), dma((4, 4)),
-            dma((4, 4)), dma((4, 4)),
+            dma((2, 8)), dma((2, 8)),
             dma((16,)), dma((16,)),
             dma((8, 2)), dma((9, 2)),
             dma((16,)), dma((16,)),

time: 99 us -> 95.6 us (0.966)
  Pallas kernels: 96.1 us -> 92.7 us
    pallas_call x1, Pallas kernels: 96.1 us -> 92.7 us  [per_device(): pl.pallas_call(kernel, out_shape=jax.ShapeDtypeStruct((16, 192, 128), f32...]
where the time goes in v6:
time: 95.6 us; the launch traced here: 95.5 us
  Pallas kernels  92.7 us (97%)
  local copies, waits for them, and re-layouts  2.73 us (3%)
    pallas_call x1, Pallas kernels, per_device(): pl.pallas_call(kernel, out_shape=jax.ShapeDtypeStruct((16, 192, 128), f32...  92.7 us
    reshape x1, local copies, waits for them, and re-layouts, per_device(): return jnp.transpose(out, (0, 2, 1)).reshape(2048, 192)  2.73 us

profile of v6, /device:TPU:1, one launch (start us, length us, event | category | flops | bytes accessed | tf_op | source)
XLA Modules:
  0.0 95.5 jit_solution(9630241185938680530)
XLA Ops:
  0.0 92.7 %whiten.1 = f32[16,192,128]{2,1,0:T(8,128)} custom-call(f32[192,2048]{1,0:T(8,128)} %bitcast.7, f32[5,64,2048]{2,1,0:T(8,128)} %fac.1, f32[5,64,1024]{2,1,0:T(8,128)} %dinv.1), custom_call_target="tpu_custom_call" | custom-call | tf_op jit(solution)/shard_map/whiten/pallas_call | solution.py:583
  92.7 2.7 %copy_bitcast_fusion = f32[2048,192]{0,1:T(8,128)} fusion(f32[16,192,128]{2,1,0:T(8,128)} %whiten.1), kind=kLoop, calls=%fused_computation | loop fusion | bytes 3145728 | tf_op jit(solution)/shard_map/reshape | solution.py:634

commit v7 on v6

--- a/solution.py
+++ b/solution.py
@@ -497,8 +497,12 @@
         updated = js[b] - total
         og[b * 8 + z] = jnp.where(block < 5, solved, updated)
         w = ways[b]
-        for k, d in enumerate((2 * w, -2 * w, w, -w)):
+        for k, d in enumerate((2 * w, -2 * w)):
             hop(b, k, z, d)
+    for b in range(2):
+        w = ways[b]
+        for k, d in enumerate((w, -w)):
+            hop(b, 2 + k, z, d)
     done = [(0, z), (1, z)]
     shared = []
 

time: 95.6 us -> 95.2 us (level)
  no operation moved by 1% of the time
where the time goes in v7:
time: 95.2 us; the launch traced here: 95 us
  Pallas kernels  92.3 us (97%)
  local copies, waits for them, and re-layouts  2.73 us (3%)
    pallas_call x1, Pallas kernels, per_device(): pl.pallas_call(kernel, out_shape=jax.ShapeDtypeStruct((16, 192, 128), f32...  92.3 us
    reshape x1, local copies, waits for them, and re-layouts, per_device(): return jnp.transpose(out, (0, 2, 1)).reshape(2048, 192)  2.73 us

profile of v7, /device:TPU:1, one launch (start us, length us, event | category | flops | bytes accessed | tf_op | source)
XLA Modules:
  0.0 95.0 jit_solution(3858695782405722180)
XLA Ops:
  0.0 92.3 %whiten.1 = f32[16,192,128]{2,1,0:T(8,128)} custom-call(f32[192,2048]{1,0:T(8,128)} %bitcast.7, f32[5,64,2048]{2,1,0:T(8,128)} %fac.1, f32[5,64,1024]{2,1,0:T(8,128)} %dinv.1), custom_call_target="tpu_custom_call" | custom-call | tf_op jit(solution)/shard_map/whiten/pallas_call | solution.py:587
  92.3 2.7 %copy_bitcast_fusion = f32[2048,192]{0,1:T(8,128)} fusion(f32[16,192,128]{2,1,0:T(8,128)} %whiten.1), kind=kLoop, calls=%fused_computation | loop fusion | bytes 3145728 | tf_op jit(solution)/shard_map/reshape | solution.py:638
